TPU v7x, 32 devices: a whole 2x2x4 slice. The times are simulated.
32 devices in a mesh: col: 8 (over z, y), row: 4 (over x, core).
Axes of the slice: x: 2, y: 2, z: 4, core: 2. Of those that a mesh axis runs over, the one named last changes fastest.
Arguments:
- panel: int32 [8], replicated, may hold values from 0 to 7, each once
- centres_cols: bfloat16 [4096, 1024], P('col'), may hold values from -1 to 1
- centres_rows: bfloat16 [128, 1024], P(('row', 'col')), may hold values from -1 to 1
- diag_inverse: float32 [4096, 512], P('col'), as said below
- trailing: float32 [128, 4096], P('row', 'col'), may hold values from -6 to 6
Outputs:
- updated: float32 [128, 4096], P('row', 'col')
Inputs may be any that keep to these rules, and one draw needn't show every extreme that they name: panel holds each of 0 to 7 once. Each 512 x 512 block of diag_inverse is lower triangular with a positive diagonal.
All inputs are finite; a program needn't handle non-finite values.
Results may differ from a plain program's by a relative error of at most 0.0003.
Values may be sent and summed in bfloat16 or wider, within the bound.
A program may use at most 64 MiB of HBM per device.

v0:
```python
import functools
import math

import jax
import jax.numpy as jnp
from jax import lax
from jax.experimental import pallas as pl
from jax.experimental.pallas import tpu as pltpu
from jax.sharding import PartitionSpec as P

LAYERS = 3
EPS = 1e-06
UNITS = 4
HOP = 3
VMEM_BYTES = 63 * 2**20
MESH = pl.DeviceIdType.MESH
F32 = jnp.float32
BF16 = jnp.bfloat16
ACOS = tuple(
    v / math.pi
    for v in (
        1.5707963050, -0.2145988016, 0.0889789874, -0.0501743046,
        0.0308918810, -0.0170881256, 0.0066700901, -0.0012624911,
    )
)


def root(y):
    y = jnp.maximum(y, 1e-30)
    return y * lax.rsqrt(y)


def theta_of(u):
    rho = jnp.clip(u, -1.0, 1.0)
    theta = rho
    for layer in range(LAYERS):
        size = jnp.abs(rho) if layer == 0 else rho
        poly = jnp.full_like(size, ACOS[-1])
        for coef in ACOS[-2::-1]:
            poly = poly * size + coef
        low = root(1.0 - size)
        angle = low * poly
        sine = low * root(1.0 + size)
        if layer == 0:
            zero_order = jnp.where(rho < 0.0, angle, 1.0 - angle)
        else:
            zero_order = 1.0 - angle
        rho_next = sine * (1.0 / math.pi) + zero_order * rho
        theta = theta * zero_order + rho_next
        rho = rho_next
    return theta


def dot_t(a, b, precision=None):
    return lax.dot_general(
        a, b, (((1,), (1,)), ((), ())), precision=precision, preferred_element_type=F32
    )


def split3(a):
    hi = a.astype(BF16)
    rest = a - hi.astype(F32)
    mid = rest.astype(BF16)
    return hi, mid, (rest - mid.astype(F32)).astype(BF16)


def product3(a, weights, transposed):
    m = a.shape[0]
    terms = jnp.concatenate(split3(a), axis=0)
    dims = (((1,), (1 if transposed else 0,)), ((), ()))

    def mul(count, w):
        return lax.dot_general(terms[:count * m], w, dims, preferred_element_type=F32)

    p, q, t = mul(3, weights[0]), mul(2, weights[1]), mul(1, weights[2])
    small = t + q[m:] + p[2 * m:]
    return (small + (q[:m] + p[m:2 * m])) + p[:m]


def kernel(
    n, nr, panel_hbm, x_hbm, rows_ref, inv_hbm, trail_hbm, out_ref,
    panel, x_ref, inv_ref, trail_ref,
    rows_buf, rows_all, inv3, py, pr, plft, done, across, w_out, wo, wm, wr, wl, kt, part, part_in,
    in_sem, rows_send, rows_recv, py_send, py_recv, pz_send, pz_recv, cx_send, cx_recv,
    wo_send, wo_recv, wm_send, wm_recv, wz_send, wz_recv, pt_send, pt_recv,
):
    col = lax.axis_index("col")
    row = lax.axis_index("row")
    nz = n // 2
    z, y = col // 2, col % 2
    y_mate = z * 2 + 1 - y
    right, left = lax.rem(col + 2, n), lax.rem(col + n - 2, n)
    blk, width = x_ref.shape
    half = blk // 2
    quarter = blk // nr
    share = quarter // 2
    size = share // UNITS
    per = rows_ref.shape[0]

    barrier = pltpu.get_barrier_semaphore()

    def greet(**where):
        pl.semaphore_signal(barrier, inc=1, device_id=where, device_id_type=MESH)

    for d in range(1, n):
        greet(col=lax.rem(col + d, n))
    for d in range(1, nr):
        greet(row=lax.rem(row + d, nr))
        greet(row=lax.rem(row + d, nr), col=y_mate)
    loads = [
        pltpu.make_async_copy(src, dst, in_sem.at[i])
        for i, (src, dst) in enumerate(
            ((panel_hbm, panel), (x_hbm, x_ref), (inv_hbm, inv_ref), (trail_hbm, trail_ref))
        )
    ]
    for load in loads:
        load.start()
    rows_buf[col] = rows_ref[...].astype(F32)
    pl.semaphore_wait(barrier, n - 1 + 2 * (nr - 1))

    def remote(src, dst, send, recv, **where):
        return pltpu.make_async_remote_copy(
            src_ref=src, dst_ref=dst, send_sem=send, recv_sem=recv,
            device_id=where, device_id_type=MESH,
        )

    def rows_copy(d, slot):
        return remote(
            rows_buf.at[slot], rows_buf.at[slot], rows_send.at[d], rows_recv.at[slot],
            col=lax.rem(col + d, n),
        )

    for d in range(1, n):
        rows_copy(d, col).start()

    def unit(k):
        return pl.ds(pl.multiple_of(k * size, size), size)

    def own_unit(side, k):
        return pl.ds(pl.multiple_of(row * quarter + side * share + k * size, size), size)

    def py_copy(k):
        return remote(
            x_hbm.at[own_unit(1 - y, k)], py.at[unit(k)], py_send.at[k], py_recv.at[k], col=y_mate
        )

    def cx_copy(k):
        return remote(
            done.at[unit(k)], across.at[unit(k)], cx_send.at[k], cx_recv.at[k], col=y_mate
        )

    for k in range(UNITS):
        py_copy(k).start()
    for load in loads:
        load.wait()

    target = n // 4
    at = jnp.int32(0)
    for i in range(n):
        at = at + jnp.where(panel[i] == target, i, 0)
    root_here = at == col
    root_layer = at // 2 == z
    from_left = at // 2 <= z

    sums = jnp.zeros((blk, 128), F32)
    for j in range(0, width, 128):
        piece = x_ref[:, j:j + 128].astype(F32)
        sums = sums + piece * piece
    x_norm = jnp.sqrt(jnp.sum(sums.T, axis=0, keepdims=True) + EPS)
    x_inv = 1.0 / x_norm
    for i, term in enumerate(split3(inv_ref[...])):
        inv3[i] = term

    def block_kernel(a, a_f):
        a_norm = jnp.sqrt(jnp.sum(a_f * a_f, axis=1, keepdims=True) + EPS)
        u = dot_t(a, x_ref[...]) * (1.0 / a_norm) * x_inv
        return theta_of(u) * (a_norm * x_norm)

    def z_copy(buf, index, k, way, send, recv):
        return remote(
            buf.at[index], buf.at[index], send.at[way, k], recv.at[way, k],
            col=right if way == 0 else left,
        )

    def position(way):
        return z if way == 0 else nz - 1 - z

    def pass_on(buf, index, k, way, cand, send, recv):
        pos = position(way)

        @pl.when(pos == 0)
        def _():
            buf[index] = cand()

        @pl.when(pos > 0)
        def _():
            z_copy(buf, index, k, way, send, recv).wait_recv()
            buf[index] = lax.select(root_layer, cand(), buf[index])

        @pl.when(pos < nz - 1)
        def _():
            z_copy(buf, index, k, way, send, recv).start()

    def panel_slot(step):
        @pl.when(step < UNITS)
        def _():
            py_copy(step).wait_recv()
            own = x_ref[own_unit(y, step), :]
            py[unit(step), :] = lax.select(root_here, own, py[unit(step), :])

        for way, buf in enumerate((pr, plft)):
            k = step - HOP * position(way)

            @pl.when(jnp.logical_and(k >= 0, k < UNITS))
            def _():
                pass_on(buf, unit(k), k, way, lambda: py[unit(k), :], pz_send, pz_recv)

        k_done = step - HOP * (nz - 1)

        @pl.when(k_done >= 0)
        def _():
            sel = unit(k_done)
            done[sel, :] = lax.select(from_left, pr[sel, :], plft[sel, :])
            cx_copy(k_done).start()

    def slots(first, last):
        @pl.loop(first, last)
        def _(step):
            panel_slot(step)

    def panel_half(side, a):
        kt[pl.ds(pl.multiple_of(side * share, share), share), :] = block_kernel(a, a.astype(F32))

    def work_rows():
        for d in range(1, n):
            slot = lax.rem(col + n - d, n)
            rows_copy(d, slot).wait_recv()
        for c in range(n):
            rows_all[c * per:(c + 1) * per, :] = rows_buf[c]
        a_f = rows_all[...]
        return block_kernel(a_f.astype(BF16), a_f)

    def wo_copy(d, slot):
        peer = lax.rem(row + d, nr)
        return remote(w_out.at[peer], wo.at[slot], wo_send.at[d], wo_recv.at[slot], row=peer)

    def wm_copy(d, slot):
        peer = lax.rem(row + d, nr)
        return remote(
            w_out.at[peer], wm.at[slot], wm_send.at[d], wm_recv.at[slot], row=peer, col=y_mate
        )

    def work_mid(a):
        low = product3(a[:, :half], [inv3[i, :half, :half] for i in range(3)], True)
        high = product3(a, [inv3[i, half:, :] for i in range(3)], True)
        return jnp.concatenate([low, high], axis=1)

    def work_w(mid):
        low = product3(mid, [inv3[i, :, :half] for i in range(3)], False)
        high = product3(mid[:, half:], [inv3[i, half:, half:] for i in range(3)], False)
        w = jnp.concatenate([low, high], axis=1)
        for j in range(nr):
            w_out[j] = w[:, j * quarter:(j + 1) * quarter]
        for d in range(nr):
            wm_copy(d, row).start()
        for d in range(1, nr):
            wo_copy(d, row).start()
        wo[row] = w_out[row]

    def work_exchange():
        for d in range(nr):
            slot = lax.rem(row + nr - d, nr)
            wm_copy(d, slot).wait_recv()
        for d in range(1, nr):
            slot = lax.rem(row + nr - d, nr)
            wo_copy(d, slot).wait_recv()
        for k in range(nr):
            wm[k] = lax.select(root_here, wo[k], wm[k])

    def w_hop(step):
        for way, buf in enumerate((wr, wl)):
            @pl.when(position(way) == step)
            def _():
                for k in range(nr):
                    pass_on(buf, k, k, way, lambda: wm[k], wz_send, wz_recv)

    last = UNITS + HOP * (nz - 1)
    slots(0, 2)
    k_rows = work_rows()
    slots(2, 4)
    mid = work_mid(k_rows)
    slots(4, 6)
    work_w(mid)
    slots(6, 8)
    work_exchange()
    w_hop(0)
    slots(8, last - 3)
    w_hop(1)
    slots(last - 3, last - 1)
    w_hop(2)
    slots(last - 1, last)
    panel_half(y, done[...])
    for k in range(UNITS):
        cx_copy(k).wait_recv()
    panel_half(1 - y, across[...])

    @pl.loop(3, nz)
    def _(step):
        w_hop(step)

    def part_copy(d, slot):
        peer = lax.rem(row + d, nr)
        return remote(part.at[peer], part_in.at[slot], pt_send.at[d], pt_recv.at[slot], row=peer)

    w = jnp.concatenate([lax.select(from_left, wr[j], wl[j]) for j in range(nr)], axis=0)
    update = jnp.dot(w, kt[...], precision=lax.Precision.HIGHEST, preferred_element_type=F32)
    group = update.shape[0] // nr
    for j in range(nr):
        part[j] = update[j * group:(j + 1) * group]
    for d in range(1, nr):
        part_copy(d, row).start()
    total = part[row]
    for d in range(1, nr):
        slot = lax.rem(row + nr - d, nr)
        part_copy(d, slot).wait_recv()
        total = total + part_in[slot]
    trail = trail_ref[...]
    trail_ref[...] = lax.select(panel[col] > target, trail - total, trail)
    store = pltpu.make_async_copy(trail_ref, out_ref, in_sem.at[0])
    store.start()

    for d in range(1, n):
        rows_copy(d, col).wait_send()
    for k in range(UNITS):
        py_copy(k).wait_send()
        cx_copy(k).wait_send()
    for d in range(nr):
        wm_copy(d, row).wait_send()
    for d in range(1, nr):
        wo_copy(d, row).wait_send()
        part_copy(d, row).wait_send()
    for way in (0, 1):
        @pl.when(position(way) < nz - 1)
        def _():
            for k in range(UNITS):
                z_copy((pr, plft)[way], unit(k), k, way, pz_send, pz_recv).wait_send()
            for k in range(nr):
                z_copy((wr, wl)[way], k, k, way, wz_send, wz_recv).wait_send()
    store.wait()


def on_device(n, nr, panel, centres_cols, centres_rows, diag_inverse, trailing):
    blk, width = centres_cols.shape
    quarter = blk // nr
    per = centres_rows.shape[0]
    group = per * n
    dma = pltpu.SemaphoreType.DMA
    vmem = pl.BlockSpec(memory_space=pltpu.VMEM)
    hbm = pl.BlockSpec(memory_space=pltpu.HBM)
    return pl.pallas_call(
        functools.partial(kernel, n, nr),
        out_shape=jax.ShapeDtypeStruct(trailing.shape, F32),
        in_specs=[hbm, hbm, vmem, hbm, hbm],
        out_specs=hbm,
        scratch_shapes=[
            pltpu.SMEM(panel.shape, jnp.int32),
            pltpu.VMEM(centres_cols.shape, BF16),
            pltpu.VMEM(diag_inverse.shape, F32),
            pltpu.VMEM(trailing.shape, F32),
            pltpu.VMEM((n, per, width), F32),
            pltpu.VMEM((group, width), F32),
            pltpu.VMEM((3, blk, blk), BF16),
            pltpu.VMEM((quarter // 2, width), BF16),
            pltpu.VMEM((quarter // 2, width), BF16),
            pltpu.VMEM((quarter // 2, width), BF16),
            pltpu.VMEM((quarter // 2, width), BF16),
            pltpu.VMEM((quarter // 2, width), BF16),
            pltpu.VMEM((nr, group, quarter), F32),
            pltpu.VMEM((nr, group, quarter), F32),
            pltpu.VMEM((nr, group, quarter), F32),
            pltpu.VMEM((nr, group, quarter), F32),
            pltpu.VMEM((nr, group, quarter), F32),
            pltpu.VMEM((quarter, blk), F32),
            pltpu.VMEM((nr, group, blk), F32),
            pltpu.VMEM((nr, group, blk), F32),
            dma((4,)),
            dma((n,)), dma((n,)),
            dma((UNITS,)), dma((UNITS,)),
            dma((2, UNITS)), dma((2, UNITS)),
            dma((UNITS,)), dma((UNITS,)),
            dma((nr,)), dma((nr,)),
            dma((nr,)), dma((nr,)),
            dma((2, nr)), dma((2, nr)),
            dma((nr,)), dma((nr,)),
        ],
        compiler_params=pltpu.CompilerParams(
            collective_id=0, has_side_effects=True, vmem_limit_bytes=VMEM_BYTES
        ),
    )(panel, centres_cols, centres_rows, diag_inverse, trailing)


def solution(mesh):
    return jax.shard_map(
        functools.partial(on_device, mesh.shape["col"], mesh.shape["row"]),
        mesh=mesh,
        in_specs=(P(), P("col", None), P(("row", "col"), None), P("col", None), P("row", "col")),
        out_specs=P("row", "col"),
        check_vma=False,
    )
```

profile of v0, /device:TPU:1, one launch (start us, length us, event | category | flops | bytes accessed | tf_op | source)
XLA Modules:
  0.0 33.7 jit_solution(10020774983413114240)
XLA Ops:
  0.0 32.2 %shard_map.55 = f32[32,512]{1,0:T(8,128)} custom-call(s32[8]{0:T(128)} %panel_hbm.1, bf16[512,1024]{1,0:T(8,128)(2,1)} %x_hbm.1, bf16[4,1024]{1,0:T(4,128)(2,1)} %rows_ref.1, f32[512,512]{1,0:T(8,128)} %inv_hbm.1, f32[32,512]{1,0:T(8,128)} %trail_hbm.1), custom_call_target="tpu_custom_call" | custom-call | tf_op jit(solution)/shard_map/pallas_call | solution.py:360
  32.2 1.5 %copy.7 = f32[32,512]{1,0:T(8,128)} copy(f32[32,512]{1,0:T(8,128)} %shard_map.55) | data formatting | bytes 131072
where the time goes:
time: 33.9 us; the launch traced here: 33.7 us
  Pallas kernels  32.2 us (95%)
  local copies, waits for them, and re-layouts  1.47 us (4%)
    pallas_call x1, Pallas kernels, on_device(): pl.pallas_call(functools.partial(kernel, n, nr), out_shape=jax.ShapeDtype...  32.2 us
    unnamed x1, local copies, waits for them, and re-layouts  1.47 us

commit v1 on v0

--- a/solution.py
+++ b/solution.py
@@ -11,7 +11,7 @@
 LAYERS = 3
 EPS = 1e-06
 UNITS = 4
-HOP = 3
+HOP = UNITS
 VMEM_BYTES = 63 * 2**20
 MESH = pl.DeviceIdType.MESH
 F32 = jnp.float32
@@ -162,18 +162,9 @@
     root_layer = at // 2 == z
     from_left = at // 2 <= z
 
-    sums = jnp.zeros((blk, 128), F32)
-    for j in range(0, width, 128):
-        piece = x_ref[:, j:j + 128].astype(F32)
-        sums = sums + piece * piece
-    x_norm = jnp.sqrt(jnp.sum(sums.T, axis=0, keepdims=True) + EPS)
-    x_inv = 1.0 / x_norm
-    for i, term in enumerate(split3(inv_ref[...])):
-        inv3[i] = term
-
-    def block_kernel(a, a_f):
+    def block_kernel(a, a_f, x_norm):
         a_norm = jnp.sqrt(jnp.sum(a_f * a_f, axis=1, keepdims=True) + EPS)
-        u = dot_t(a, x_ref[...]) * (1.0 / a_norm) * x_inv
+        u = dot_t(a, x_ref[...]) * (1.0 / a_norm) * (1.0 / x_norm)
         return theta_of(u) * (a_norm * x_norm)
 
     def z_copy(buf, index, k, way, send, recv):
@@ -229,7 +220,7 @@
             panel_slot(step)
 
     def panel_half(side, a):
-        kt[pl.ds(pl.multiple_of(side * share, share), share), :] = block_kernel(a, a.astype(F32))
+        kt[pl.ds(pl.multiple_of(side * share, share), share), :] = block_kernel(a, a.astype(F32), x_norm)
 
     def work_rows():
         for d in range(1, n):
@@ -238,7 +229,7 @@
         for c in range(n):
             rows_all[c * per:(c + 1) * per, :] = rows_buf[c]
         a_f = rows_all[...]
-        return block_kernel(a_f.astype(BF16), a_f)
+        return block_kernel(a_f.astype(BF16), a_f, x_norm)
 
     def wo_copy(d, slot):
         peer = lax.rem(row + d, nr)
@@ -284,22 +275,26 @@
                 for k in range(nr):
                     pass_on(buf, k, k, way, lambda: wm[k], wz_send, wz_recv)
 
-    last = UNITS + HOP * (nz - 1)
-    slots(0, 2)
+    slots(0, HOP)
+
+    sums = jnp.zeros((blk, 128), F32)
+    for j in range(0, width, 128):
+        piece = x_ref[:, j:j + 128].astype(F32)
+        sums = sums + piece * piece
+    x_norm = jnp.sqrt(jnp.sum(sums.T, axis=0, keepdims=True) + EPS)
+    for i, term in enumerate(split3(inv_ref[...])):
+        inv3[i] = term
+
     k_rows = work_rows()
-    slots(2, 4)
-    mid = work_mid(k_rows)
-    slots(4, 6)
-    work_w(mid)
-    slots(6, 8)
+    slots(HOP, 2 * HOP)
+    work_w(work_mid(k_rows))
+    slots(2 * HOP, 3 * HOP)
     work_exchange()
     w_hop(0)
-    slots(8, last - 3)
+    slots(3 * HOP, nz * HOP)
     w_hop(1)
-    slots(last - 3, last - 1)
+    panel_half(y, done[...])
     w_hop(2)
-    slots(last - 1, last)
-    panel_half(y, done[...])
     for k in range(UNITS):
         cx_copy(k).wait_recv()
     panel_half(1 - y, across[...])

time: 33.9 us -> 33.7 us (level)
  no operation moved by 1% of the time
where the time goes in v1:
time: 33.7 us; the launch traced here: 33.5 us
  Pallas kernels  32 us (95%)
  local copies, waits for them, and re-layouts  1.47 us (4%)
    pallas_call x1, Pallas kernels, on_device(): pl.pallas_call(functools.partial(kernel, n, nr), out_shape=jax.ShapeDtype...  32 us
    unnamed x1, local copies, waits for them, and re-layouts  1.47 us

profile of v1, /device:TPU:1, one launch (start us, length us, event | category | flops | bytes accessed | tf_op | source)
XLA Modules:
  0.0 33.5 jit_solution(7701719161803832257)
XLA Ops:
  0.0 32.0 %shard_map.55 = f32[32,512]{1,0:T(8,128)} custom-call(s32[8]{0:T(128)} %panel_hbm.1, bf16[512,1024]{1,0:T(8,128)(2,1)} %x_hbm.1, bf16[4,1024]{1,0:T(4,128)(2,1)} %rows_ref.1, f32[512,512]{1,0:T(8,128)} %inv_hbm.1, f32[32,512]{1,0:T(8,128)} %trail_hbm.1), custom_call_target="tpu_custom_call" | custom-call | tf_op jit(solution)/shard_map/pallas_call | solution.py:355
  32.0 1.5 %copy.7 = f32[32,512]{1,0:T(8,128)} copy(f32[32,512]{1,0:T(8,128)} %shard_map.55) | data formatting | bytes 131072
